TPU v7x, 32 devices: a whole 2x2x4 slice. The times are simulated.
32 devices in a mesh: row: 4 (over y, x), col: 8 (over z, core).
Axes of the slice: x: 2, y: 2, z: 4, core: 2. Of those that a mesh axis runs over, the one named last changes fastest.
Arguments:
- tokens: bfloat16 [128, 12288], P('col', 'row'), may hold values from -6 to 6
- w_in: bfloat16 [12288, 24576], P('row', 'col'), may hold values from -0.0546875 to 0.0546875
- w_out: bfloat16 [24576, 12288], P('col', 'row'), may hold values from -0.0390625 to 0.0390625
- grad_out: bfloat16 [128, 12288], P('col', 'row'), may hold values from -6 to 6
Outputs:
- block_out: bfloat16 [128, 12288], P('col', 'row')
- grad_tokens: bfloat16 [128, 12288], P('col', 'row')
- grad_w_in: bfloat16 [12288, 24576], P('row', 'col')
- grad_w_out: bfloat16 [24576, 12288], P('col', 'row')
All inputs are finite; a program needn't handle non-finite values.
Results may differ from a plain program's by a relative error of at most 0.02.
Values may be sent and summed in bfloat16 or wider, within the bound.
A program may use at most 192 MiB of HBM per device.

v0:
```python
import jax
import jax.numpy as jnp
from jax import lax
from jax.sharding import PartitionSpec as P

gelu_scale = 0.7978845608028654
gelu_cubic = 0.044715


def gelu_pair(value):
    inner = gelu_scale * (value + gelu_cubic * value * value * value)
    tangent = jnp.tanh(inner)
    result = 0.5 * value * (1.0 + tangent)
    slope = 0.5 * (1.0 + tangent) + 0.5 * value * (1.0 - tangent * tangent) * gelu_scale * (
        1.0 + 3.0 * gelu_cubic * value * value
    )
    return (result, slope)


def activate(pre, grad_hidden):
    result, slope = gelu_pair(pre)
    return (result.astype(jnp.bfloat16), (grad_hidden * slope).astype(jnp.bfloat16))


def per_device(tokens, w_in, w_out, grad_out):
    token_panel, grad_panel = (
        lax.all_gather(tokens, "col", axis=0, tiled=True),
        lax.all_gather(grad_out, "col", axis=0, tiled=True),
    )
    pre_terms = jnp.dot(token_panel, w_in, preferred_element_type=jnp.float32)
    hidden_terms = lax.dot_general(
        grad_panel, w_out, (((1,), (1,)), ((), ())), preferred_element_type=jnp.float32
    )
    pre, grad_hidden = (
        lax.psum_scatter(
            pre_terms.astype(jnp.bfloat16), "row", scatter_dimension=0, tiled=True
        ).astype(jnp.float32),
        lax.psum_scatter(
            hidden_terms.astype(jnp.bfloat16), "row", scatter_dimension=0, tiled=True
        ).astype(jnp.float32),
    )
    hidden, grad_pre = activate(pre, grad_hidden)
    hidden_full, grad_pre_full = (
        lax.all_gather(hidden, "row", axis=0, tiled=True),
        lax.all_gather(grad_pre, "row", axis=0, tiled=True),
    )
    out_terms = jnp.dot(hidden_full, w_out, preferred_element_type=jnp.float32)
    input_terms = lax.dot_general(
        grad_pre_full, w_in, (((1,), (1,)), ((), ())), preferred_element_type=jnp.float32
    )
    block_out, grad_tokens = (
        lax.psum_scatter(
            out_terms.astype(jnp.bfloat16), "col", scatter_dimension=0, tiled=True
        ).astype(jnp.float32),
        lax.psum_scatter(
            input_terms.astype(jnp.bfloat16), "col", scatter_dimension=0, tiled=True
        ).astype(jnp.float32),
    )
    grad_w_in = lax.dot_general(
        token_panel, grad_pre_full, (((0,), (0,)), ((), ())), preferred_element_type=jnp.float32
    )
    grad_w_out = lax.dot_general(
        hidden_full, grad_panel, (((0,), (0,)), ((), ())), preferred_element_type=jnp.float32
    )
    return (
        block_out.astype(jnp.bfloat16),
        grad_tokens.astype(jnp.bfloat16),
        grad_w_in.astype(jnp.bfloat16),
        grad_w_out.astype(jnp.bfloat16),
    )


def solution(mesh):
    placed = (P("col", "row"), P("row", "col"), P("col", "row"), P("col", "row"))
    return jax.shard_map(
        per_device,
        mesh=mesh,
        in_specs=placed,
        out_specs=(P("col", "row"), P("col", "row"), P("row", "col"), P("col", "row")),
        check_vma=False,
    )
```

profile of v0, /device:TPU:0, one launch (start us, length us, event | category | flops | bytes accessed | tf_op | source)
XLA Modules:
  0.0 192.7 jit_solution(10235182018453485376)
XLA Ops:
  7.2 0.0 copy-start
  7.2 0.0 reduce-scatter.9.cloned.1.call-start
  7.2 17.4 %all_gather.14 = bf16[128,3072]{1,0:T(8,128)(2,1)S(1)} all-gather(bf16[16,3072]{1,0:T(8,128)(2,1)} %param.7), channel_id=1, replica_groups=mesh['row'=4,'col'=8] {'col'}, dimensions={0}, use_global_device_ids=true | all-gather | bytes 884736 | tf_op jit(solution)/shard_map/all_gather | solution.py:28
  24.7 13.6 %convolution_convert_fusion.2 = bf16[128,3072]{1,0:T(8,128)(2,1)} fusion(bf16[128,3072]{1,0:T(8,128)(2,1)S(1)} %all_gather.14, bf16[3072,3072]{1,0:T(8,128)(2,1)} %param.6), kind=kOutput, calls=%fused_computation.3 | convolution fusion | flops 2416312320 | bytes 20447232 | tf_op jit(solution)/shard_map/dot_general | solution.py:31
  38.2 0.0 reduce-scatter.9.cloned.1.call-update
  38.2 0.0 reduce-scatter.5.cloned.1.call-start
  38.3 0.0 copy-done
  38.3 15.7 %all_gather.12 = bf16[128,3072]{1,0:T(8,128)(2,1)S(1)} all-gather(bf16[16,3072]{1,0:T(8,128)(2,1)S(1)} %copy-done), channel_id=1, replica_groups=mesh['row'=4,'col'=8] {'col'}, dimensions={0}, use_global_device_ids=true | all-gather | bytes 884736 | tf_op jit(solution)/shard_map/all_gather | solution.py:27
  54.0 9.9 %convolution_convert_fusion.4 = bf16[128,3072]{1,0:T(8,128)(2,1)} fusion(bf16[128,3072]{1,0:T(8,128)(2,1)S(1)} %all_gather.12, bf16[3072,3072]{1,0:T(8,128)(2,1)} %param.5), kind=kOutput, calls=%fused_computation.5 | convolution fusion | flops 2416312320 | bytes 20447232 | tf_op jit(solution)/shard_map/dot_general | solution.py:30
  63.9 0.0 reduce-scatter.5.cloned.1.call-update
  63.9 0.0 reduce-scatter.7.cloned.1.call-start
  64.0 1.7 reduce-scatter.9.cloned.1.call-done
  65.7 29.6 %reduce-scatter.5.cloned.1.call-done = bf16[32,3072]{1,0:T(8,128)(2,1)} async-done(((bf16[128,3072]{1,0:T(8,128)(2,1)}), bf16[32,3072]{1,0:T(8,128)(2,1)}) %reduce-scatter.5.cloned.1.call-update) | async-done | bytes 196624 | tf_op jit(solution)/shard_map/reduce_scatter | solution.py:35
  95.3 1.3 fusion.7
  96.6 11.1 %all_gather.13 = bf16[128,3072]{1,0:T(8,128)(2,1)S(1)} all-gather(bf16[32,3072]{1,0:T(8,128)(2,1)S(1)} %get-tuple-element.9), channel_id=1, replica_groups=mesh['row'=4,'col'=8] {'row'}, dimensions={0}, use_global_device_ids=true | all-gather | bytes 983040 | tf_op jit(solution)/shard_map/all_gather | solution.py:44
  107.7 9.9 %convolution_convert_fusion.3 = bf16[128,3072]{1,0:T(8,128)(2,1)} fusion(bf16[128,3072]{1,0:T(8,128)(2,1)S(1)} %all_gather.13, bf16[3072,3072]{1,0:T(8,128)(2,1)} %param.6), kind=kOutput, calls=%fused_computation.4 | convolution fusion | flops 2416312320 | bytes 20447232 | tf_op jit(solution)/shard_map/dot_general | solution.py:47
  117.6 0.0 reduce-scatter.7.cloned.1.call-update
  117.6 0.0 reduce-scatter.11.cloned.1.call-start
  117.7 11.2 %all_gather.15 = bf16[128,3072]{1,0:T(8,128)(2,1)S(1)} all-gather(bf16[32,3072]{1,0:T(8,128)(2,1)S(1)} %get-tuple-element.8), channel_id=1, replica_groups=mesh['row'=4,'col'=8] {'row'}, dimensions={0}, use_global_device_ids=true | all-gather | bytes 983040 | tf_op jit(solution)/shard_map/all_gather | solution.py:45
  128.9 13.6 %convolution_convert_fusion.1 = bf16[128,3072]{1,0:T(8,128)(2,1)} fusion(bf16[128,3072]{1,0:T(8,128)(2,1)S(1)} %all_gather.15, bf16[3072,3072]{1,0:T(8,128)(2,1)} %param.5), kind=kOutput, calls=%fused_computation.2 | convolution fusion | flops 2416312320 | bytes 20447232 | tf_op jit(solution)/shard_map/dot_general | solution.py:48
  142.5 0.0 reduce-scatter.11.cloned.1.call-update
  142.5 9.5 %convert_bitcast_fusion = bf16[3072,3072]{0,1:T(8,128)(2,1)} fusion(bf16[128,3072]{1,0:T(8,128)(2,1)S(1)} %all_gather.15, bf16[128,3072]{1,0:T(8,128)(2,1)S(1)} %all_gather.12), kind=kOutput, calls=%fused_computation | convolution fusion | flops 2425356288 | bytes 20447232 | tf_op jit(solution)/shard_map/dot_general | solution.py:59
  152.1 24.6 %copy.8 = bf16[3072,3072]{1,0:T(8,128)(2,1)} copy(bf16[3072,3072]{0,1:T(8,128)(2,1)} %convert_bitcast_fusion) | data formatting | bytes 37748736
  176.7 9.5 %convolution_convert_fusion = bf16[3072,3072]{1,0:T(8,128)(2,1)} fusion(bf16[128,3072]{1,0:T(8,128)(2,1)S(1)} %all_gather.13, bf16[128,3072]{1,0:T(8,128)(2,1)S(1)} %all_gather.14), kind=kOutput, calls=%fused_computation.1 | convolution fusion | flops 2425356288 | bytes 20447232 | tf_op jit(solution)/shard_map/dot_general | solution.py:62
  186.1 0.0 reduce-scatter.7.cloned.1.call-done
  186.2 0.0 reduce-scatter.11.cloned.1.call-done
Async XLA Ops:
  7.2 31.1 %copy-start = (bf16[16,3072]{1,0:T(8,128)(2,1)S(1)}, bf16[16,3072]{1,0:T(8,128)(2,1)}, u32[]{:S(2)}) copy-start(bf16[16,3072]{1,0:T(8,128)(2,1)} %param.4) | copy-start | bytes 294916
  7.2 58.5 %reduce-scatter.9.cloned.1.call-start = ((), (), s32[]{:S(2)}) async-start(), calls=%async_computation.6 | async-start | bytes 983040 | tf_op jit(solution)/shard_map/reduce_scatter | solution.py:38
  38.2 57.1 %reduce-scatter.5.cloned.1.call-start = ((), (), s32[]{:S(2)}) async-start(), calls=%async_computation.4 | async-start | bytes 983040 | tf_op jit(solution)/shard_map/reduce_scatter | solution.py:35
  63.9 122.2 %reduce-scatter.7.cloned.1.call-start = ((), (), s32[]{:S(2)}) async-start(), calls=%async_computation.5 | async-start | bytes 884736 | tf_op jit(solution)/shard_map/reduce_scatter | solution.py:52
  117.6 68.5 %reduce-scatter.11.cloned.1.call-start = ((), (), s32[]{:S(2)}) async-start(), calls=%async_computation.7 | async-start | bytes 884736 | tf_op jit(solution)/shard_map/reduce_scatter | solution.py:55
Sparse Core Ops, SparseCore 0:
  38.4 27.3 reduce-scatter.8
  69.2 26.0 reduce-scatter.4
  117.7 31.4 reduce-scatter.6
  152.1 29.7 reduce-scatter.10
where the time goes:
time: 194 us; the launch traced here: 193 us
  matrix products  66 us (34%)
  blocking collectives  55.4 us (29%)
  waiting for transfers between devices  31.4 us (16%)
  local copies, waits for them, and re-layouts  24.6 us (13%)
  between operations  13.8 us (7%)
    reduce_scatter x1, waiting for transfers between devices, per_device(): lax.psum_scatter(pre_terms.astype(jnp.bfloat16), 'row', scatter_dimension...  29.6 us
    unnamed x3, local copies, waits for them, and re-layouts  24.6 us
    all_gather x1, blocking collectives, per_device(): lax.all_gather(grad_out, 'col', axis=0, tiled=True)  17.4 us
    all_gather x1, blocking collectives, per_device(): lax.all_gather(tokens, 'col', axis=0, tiled=True)  15.7 us
    dot_general x1, matrix products, per_device(): lax.dot_general(grad_pre_full, w_in, (((1,), (1,)), ((), ())), preferred_...  13.6 us
    dot_general x1, matrix products, per_device(): lax.dot_general(grad_panel, w_out, (((1,), (1,)), ((), ())), preferred_el...  13.6 us
    all_gather x1, blocking collectives, per_device(): lax.all_gather(grad_pre, 'row', axis=0, tiled=True)  11.2 us
    all_gather x1, blocking collectives, per_device(): lax.all_gather(hidden, 'row', axis=0, tiled=True)  11.1 us
  transfers between devices with their start and end apart: 4, of which 2 were waited for; matrix products, arithmetic and copies ran while one was open for 35% of the time, Pallas kernels for 0%

commit v1 on v0

v1 whole, which is shorter than its diff:
```python
import functools

import jax
import jax.numpy as jnp
from jax import lax
from jax.experimental import pallas as pl
from jax.experimental.pallas import tpu as pltpu
from jax.sharding import PartitionSpec as P

gelu_scale = 0.7978845608028654
gelu_cubic = 0.044715
TILE = 256
F32 = jnp.float32
BF16 = jnp.bfloat16


def gelu_pair(value):
    inner = gelu_scale * (value + gelu_cubic * value * value * value)
    tangent = jnp.tanh(inner)
    result = 0.5 * value * (1.0 + tangent)
    slope = 0.5 * (1.0 + tangent) + 0.5 * value * (1.0 - tangent * tangent) * gelu_scale * (
        1.0 + 3.0 * gelu_cubic * value * value
    )
    return (result, slope)


def aligned(index, size):
    return pl.ds(pl.multiple_of(index * size, size), size)


def dot_nt(left, right):
    return lax.dot_general(left, right, (((1,), (1,)), ((), ())), preferred_element_type=F32)


def kernel(
    n_row, n_col, chunk, part,
    x_ref, g_ref, w_in_hbm, w_out_hbm,
    out_ref, gt_ref, xp, gp, hid, gpre,
    w_in, w_out, terms_a, terms_b, land_a, land_b, slope, total, own_a, own_b,
    pair_a, pair_b, sums_a, sums_b, last_a, last_b,
    load_sem, ag_send, ag_recv, fw_send, fw_recv, rs_send, rs_recv, hg_send, hg_recv,
    pr_send, pr_recv, zs_send, zs_recv,
):
    r, q = lax.axis_index("row"), lax.axis_index("col")
    n_chip = n_col // 2
    z, core = q // 2, q % 2
    mate = z * 2 + (1 - core)
    n_tok, width = xp.shape
    hidden_units = hid.shape[1]
    n_chunk = hidden_units // chunk
    n_part = width // part
    rows_r = n_tok // n_row
    rows_c = n_tok // n_col

    def row_at(k):
        return lax.rem(r + k, n_row)

    def z_at(k):
        return lax.rem(z + k, n_chip)

    def load(which, j):
        if which == 0:
            return pltpu.make_async_copy(
                w_in_hbm.at[:, aligned(j, chunk)], w_in.at[:, aligned(j, chunk)], load_sem.at[0, j])
        return pltpu.make_async_copy(
            w_out_hbm.at[aligned(j, chunk), :], w_out.at[aligned(j, chunk), :], load_sem.at[1, j])

    for which in range(2):
        for j in range(n_chunk):
            load(which, j).start()

    barrier = pltpu.get_barrier_semaphore()
    for k in range(1, n_row):
        pl.semaphore_signal(barrier, inc=1, device_id={"row": row_at(k)}, device_id_type=pl.DeviceIdType.MESH)
    for k in range(1, n_chip):
        pl.semaphore_signal(barrier, inc=1, device_id={"col": z_at(k) * 2 + core}, device_id_type=pl.DeviceIdType.MESH)
    pl.semaphore_signal(barrier, inc=1, device_id={"col": mate}, device_id_type=pl.DeviceIdType.MESH)
    pl.semaphore_wait(barrier, n_row - 1 + n_chip - 1 + 1)

    def remote(src, dst, send, recv, **where):
        return pltpu.make_async_remote_copy(
            src_ref=src, dst_ref=dst, send_sem=send, recv_sem=recv,
            device_id=where, device_id_type=pl.DeviceIdType.MESH)

    blocks = (x_ref, g_ref)
    panels = (xp, gp)

    def gather_out(a, k):
        mine = panels[a].at[aligned(q, rows_c)]
        return remote(blocks[a], mine, ag_send.at[a, k], ag_recv.at[a, k], col=z_at(k) * 2 + core)

    def gather_in(a, k):
        there = panels[a].at[aligned(z_at(n_chip - k) * 2 + core, rows_c)]
        return remote(there, there, ag_send.at[a, k], ag_recv.at[a, k], col=mate)

    def forward_out(a, k):
        there = panels[a].at[aligned(z_at(n_chip - k) * 2 + core, rows_c)]
        source = blocks[a] if k == 0 else there
        return remote(source, there, fw_send.at[a, k], fw_recv.at[a, k], col=mate)

    def forward_in(a, k):
        there = panels[a].at[aligned(z_at(n_chip - k) * 2 + (1 - core), rows_c)]
        return remote(there, there, fw_send.at[a, k], fw_recv.at[a, k], col=mate)

    for a in range(2):
        for k in range(1, n_chip):
            gather_out(a, k).start()
        forward_out(a, 0).start()
    for a in range(2):
        panels[a][aligned(q, rows_c), :] = blocks[a][...]

    def finish_panel(a):
        for k in range(1, n_chip):
            gather_in(a, k).wait_recv()
            forward_out(a, k).start()
        for k in range(n_chip):
            forward_in(a, k).wait_recv()

    terms = (terms_a, terms_b)
    lands = (land_a, land_b)
    fulls = (hid, gpre)

    def scatter_out(a, j, k):
        to = row_at(k)
        cols = aligned(j, chunk)
        return remote(terms[a].at[aligned(to, rows_r), cols], lands[a].at[k - 1, :, cols],
                      rs_send.at[a, j, k], rs_recv.at[a, j, k], row=to)

    def spread_out(a, j, k):
        there = fulls[a].at[aligned(r, rows_r), aligned(j, chunk)]
        return remote(there, there, hg_send.at[a, j, k], hg_recv.at[a, j, k], row=row_at(k))

    def spread_in(a, j, k):
        there = fulls[a].at[aligned(row_at(n_row - k), rows_r), aligned(j, chunk)]
        return remote(there, there, hg_send.at[a, j, k], hg_recv.at[a, j, k], row=row_at(k))

    def first(a):
        def per_chunk(j, carry):
            load(a, j).wait()

            def per_tile(t, carry):
                at = aligned(j * (chunk // TILE) + t, TILE)
                if a == 0:
                    value = jnp.dot(xp[...], w_in[:, at], preferred_element_type=F32)
                else:
                    value = dot_nt(gp[...], w_out[at, :])
                terms[a][:, at] = value.astype(BF16)
                return carry

            lax.fori_loop(0, chunk // TILE, per_tile, 0)
            for k in range(1, n_row):
                scatter_out(a, j, k).start()
            return carry

        lax.fori_loop(0, n_chunk, per_chunk, 0)

    def middle(a):
        def per_chunk(j, carry):
            cols = aligned(j, chunk)
            total_here = terms[a][aligned(r, rows_r), cols].astype(F32)
            for k in range(1, n_row):
                scatter_out(a, j, k).wait_recv()
                total_here = total_here + lands[a][k - 1, :, cols].astype(F32)
            if a == 0:
                value, gradient = gelu_pair(total_here)
                slope[:, cols] = gradient
            else:
                value = total_here * slope[:, cols]
            fulls[a][aligned(r, rows_r), cols] = value.astype(BF16)
            for k in range(1, n_row):
                spread_out(a, j, k).start()
            return carry

        lax.fori_loop(0, n_chunk, per_chunk, 0)

    owns = (own_a, own_b)
    pairs = (pair_a, pair_b)
    sums = (sums_a, sums_b)
    lasts = (last_a, last_b)
    results = (out_ref, gt_ref)

    def pair_out(a, h):
        cols = pl.ds(h * part, part)
        return remote(owns[a].at[1 - core, :, cols], pairs[a].at[:, cols],
                      pr_send.at[a, h], pr_recv.at[a, h], col=mate)

    def chip_out(a, h, k):
        cols = pl.ds(h * part, part)
        to = z_at(k)
        return remote(sums[a].at[aligned(to, rows_c), cols], lasts[a].at[k - 1, :, cols],
                      zs_send.at[a, h, k], zs_recv.at[a, h, k], col=to * 2 + core)

    def second(a):
        def term(j, t):
            cols, at = aligned(j, chunk), aligned(t, TILE)
            if a == 0:
                return jnp.dot(hid[:, cols], w_out[cols, at], preferred_element_type=F32)
            return dot_nt(gpre[:, cols], w_in[at, cols])

        def arrive(j):
            for k in range(1, n_row):
                spread_in(a, j, k).wait_recv()

        def per_chunk(j, carry):
            arrive(j)

            def per_tile(t, carry):
                at = aligned(t, TILE)
                fresh = term(j, t)

                @pl.when(j == 0)
                def _():
                    total[:, at] = fresh

                @pl.when(j > 0)
                def _():
                    total[:, at] += fresh

                return carry

            lax.fori_loop(0, width // TILE, per_tile, 0)
            return carry

        lax.fori_loop(0, n_chunk - 1, per_chunk, 0)
        arrive(n_chunk - 1)
        for h in range(n_part):
            def last_tile(t, carry):
                at = aligned(t, TILE)
                value = term(n_chunk - 1, t)
                if n_chunk > 1:
                    value = total[:, at] + value
                value = value.astype(BF16).reshape(n_chip, 2, rows_c, TILE)
                for side in range(2):
                    owns[a][side, :, at] = value[:, side].reshape(n_chip * rows_c, TILE)
                return carry

            lax.fori_loop(h * (part // TILE), (h + 1) * (part // TILE), last_tile, 0)
            pair_out(a, h).start()
        for h in range(n_part):
            cols = pl.ds(h * part, part)
            pair_out(a, h).wait_recv()
            both = owns[a][core, :, cols].astype(F32) + pairs[a][:, cols].astype(F32)
            sums[a][:, cols] = both.astype(BF16)
            for k in range(1, n_chip):
                chip_out(a, h, k).start()

    def end(a):
        for h in range(n_part):
            cols = pl.ds(h * part, part)
            value = sums[a][aligned(z, rows_c), cols].astype(F32)
            for k in range(1, n_chip):
                chip_out(a, h, k).wait_recv()
                value = value + lasts[a][k - 1, :, cols].astype(F32)
            results[a][:, cols] = value.astype(BF16)

    finish_panel(0)
    first(0)
    finish_panel(1)
    first(1)
    middle(0)
    middle(1)
    second(0)
    second(1)
    end(0)
    end(1)

    for a in range(2):
        for k in range(1, n_chip):
            gather_out(a, k).wait_send()
        for k in range(n_chip):
            forward_out(a, k).wait_send()
        for h in range(n_part):
            pair_out(a, h).wait_send()
            for k in range(1, n_chip):
                chip_out(a, h, k).wait_send()

        def sent(j, carry):
            for k in range(1, n_row):
                scatter_out(a, j, k).wait_send()
                spread_out(a, j, k).wait_send()
            return carry

        lax.fori_loop(0, n_chunk, sent, 0)


def exchange(n_row, n_col, tokens, w_in, w_out, grad_out):
    rows_c, width = tokens.shape
    n_tok = rows_c * n_col
    rows_r = n_tok // n_row
    hidden_units = w_in.shape[1]
    n_chip = n_col // 2
    chunk = 768 if hidden_units % 768 == 0 else TILE
    part = 1536 if width % 1536 == 0 else width
    n_chunk, n_part = hidden_units // chunk, width // part
    shape = jax.ShapeDtypeStruct
    vmem = pl.BlockSpec(memory_space=pltpu.VMEM)
    hbm = pl.BlockSpec(memory_space=pl.ANY)
    dma = pltpu.SemaphoreType.DMA
    twice = lambda *dims: [pltpu.VMEM(dims, BF16)] * 2
    return pl.pallas_call(
        functools.partial(kernel, n_row, n_col, chunk, part),
        out_shape=(
            shape((rows_c, width), BF16), shape((rows_c, width), BF16),
            shape((n_tok, width), BF16), shape((n_tok, width), BF16),
            shape((n_tok, hidden_units), BF16), shape((n_tok, hidden_units), BF16),
        ),
        in_specs=[vmem, vmem, hbm, hbm],
        out_specs=[vmem] * 6,
        scratch_shapes=[
            pltpu.VMEM(w_in.shape, BF16), pltpu.VMEM(w_out.shape, BF16),
            *twice(n_tok, hidden_units),
            *twice(n_row - 1, rows_r, hidden_units),
            pltpu.VMEM((rows_r, hidden_units), F32),
            pltpu.VMEM((n_tok, width), F32),
            *twice(2, n_chip * rows_c, width),
            *twice(n_chip * rows_c, width),
            *twice(n_chip * rows_c, width),
            *twice(n_chip - 1, rows_c, width),
            dma((2, n_chunk)),
            dma((2, n_chip)), dma((2, n_chip)), dma((2, n_chip)), dma((2, n_chip)),
            dma((2, n_chunk, n_row)), dma((2, n_chunk, n_row)),
            dma((2, n_chunk, n_row)), dma((2, n_chunk, n_row)),
            dma((2, n_part)), dma((2, n_part)),
            dma((2, n_part, n_chip)), dma((2, n_part, n_chip)),
        ],
        compiler_params=pltpu.CompilerParams(
            collective_id=0, has_side_effects=True, vmem_limit_bytes=60 * 1024 * 1024),
        cost_estimate=pl.CostEstimate(
            flops=8 * n_tok * width * hidden_units,
            bytes_accessed=4 * width * hidden_units,
            transcendentals=rows_r * hidden_units),
        name="exchange",
    )(tokens, grad_out, w_in, w_out)


def per_device(n_row, n_col, tokens, w_in, w_out, grad_out):
    block_out, grad_tokens, token_panel, grad_panel, hidden, grad_pre = exchange(
        n_row, n_col, tokens, w_in, w_out, grad_out)
    grad_w_in = lax.dot_general(
        token_panel, grad_pre, (((0,), (0,)), ((), ())), preferred_element_type=F32)
    grad_w_out = lax.dot_general(
        hidden, grad_panel, (((0,), (0,)), ((), ())), preferred_element_type=F32)
    return (block_out, grad_tokens, grad_w_in.astype(BF16), grad_w_out.astype(BF16))


def solution(mesh):
    placed = (P("col", "row"), P("row", "col"), P("col", "row"), P("col", "row"))
    return jax.shard_map(
        functools.partial(per_device, mesh.shape["row"], mesh.shape["col"]),
        mesh=mesh,
        in_specs=placed,
        out_specs=(P("col", "row"), P("col", "row"), P("row", "col"), P("col", "row")),
        check_vma=False,
    )
```

time: 194 us -> 105 us (0.54)
  Pallas kernels: 0 us -> 82.6 us
  blocking collectives: 55.4 us -> 0 us
  matrix products: 66 us -> 20.4 us
  waiting for transfers between devices: 31.4 us -> 0 us
  local copies, waits for them, and re-layouts: 24.6 us -> 1.3 us
  between operations: 13.8 us -> 0.67 us
    pallas_call x0 -> x1, Pallas kernels: none -> 82.6 us  [exchange(): pl.pallas_call(functools.partial(kernel, n_row, n_col, chunk, part), out_...]
    all_gather x4 -> x0, blocking collectives: 55.4 us -> none  [the longest x1 17.4 us: per_device(): lax.all_gather(grad_out, 'col', axis=0, tiled=True)]
    dot_general x6 -> x2, matrix products: 66 us -> 20.4 us  [the longest x1 10.9 us: per_device(): lax.dot_general(token_panel, grad_pre, (((0,), (0,)), ((), ())), preferre...]
    reduce_scatter x4 -> x0, waiting for transfers between devices: 31.3 us -> none  [the longest x1 29.6 us: per_device(): lax.psum_scatter(pre_terms.astype(jnp.bfloat16), 'row', scatter_dimension...]
    unnamed x3 -> x10, local copies, waits for them, and re-layouts: 24.6 us -> 1.3 us
  transfers between devices with their start and end apart: 4 -> 0, of which waited for: 2 -> 0; matrix products, arithmetic and copies ran while one was open for 35% -> 0% of each run, Pallas kernels for 0% -> 0%
where the time goes in v1:
time: 105 us
  Pallas kernels  82.6 us (79%)
  matrix products  20.4 us (19%)
  local copies, waits for them, and re-layouts  1.3 us (1%)
    pallas_call x1, Pallas kernels, exchange(): pl.pallas_call(functools.partial(kernel, n_row, n_col, chunk, part), out_...  82.6 us
    dot_general x1, matrix products, per_device(): lax.dot_general(token_panel, grad_pre, (((0,), (0,)), ((), ())), preferre...  10.9 us
    dot_general x1, matrix products, per_device(): lax.dot_general(hidden, grad_panel, (((0,), (0,)), ((), ())), preferred_e...  9.51 us

profile of v1, /device:TPU:0, one launch (start us, length us, event | category | flops | bytes accessed | tf_op | source)
XLA Modules:
  0.0 105.0 jit_solution(4896311016916121364)
XLA Ops:
  0.6 82.6 %exchange.1 = (bf16[16,3072]{1,0:T(8,128)(2,1)}, bf16[16,3072]{1,0:T(8,128)(2,1)}, bf16[128,3072]{1,0:T(8,128)(2,1)}, bf16[128,3072]{1,0:T(8,128)(2,1)}, bf16[12...) custom-call(bf16[16,3072]{1,0:T(8,128)(2,1)} %x_ref.1, bf16[16,3072]{1,0:T(8,128)(2,1)} %g_ref.1, ...), custom_call_target="tpu_custom_call" | custom-call | flops 9663676416 | bytes 37748736 | tf_op jit(solution)/shard_map/exchange/pallas_call | solution.py:300
  83.3 0.0 copy-start
  83.3 0.0 copy-start.1
  83.3 10.9 %convolution_convert_fusion.1 = bf16[3072,3072]{1,0:T(8,128)(2,1)} fusion(bf16[128,3072]{1,0:T(8,128)(2,1)} %get-tuple-element.12, bf16[128,3072]{1,0:T(8,128)(2,1)} %get-tuple-element.13), kind=kOutput, calls=%fused_computation.1 | convolution fusion | flops 2425356288 | bytes 20447232 | tf_op jit(solution)/shard_map/dot_general | solution.py:339
  94.2 0.0 copy-done
  94.2 0.0 copy-done.1
  94.2 0.0 copy-start.3
  94.2 0.0 copy-start.2
  94.2 9.5 %convolution_convert_fusion = bf16[3072,3072]{1,0:T(8,128)(2,1)} fusion(bf16[128,3072]{1,0:T(8,128)(2,1)S(1)} %copy-done, bf16[128,3072]{1,0:T(8,128)(2,1)S(1)} %copy-done.1), kind=kOutput, calls=%fused_computation | convolution fusion | flops 2425356288 | bytes 20447232 | tf_op jit(solution)/shard_map/dot_general | solution.py:341
  103.7 0.0 copy-done.3
  103.7 0.6 copy.10
  104.4 0.0 copy-done.2
  104.4 0.6 copy.11
Async XLA Ops:
  83.3 10.9 %copy-start = (bf16[128,3072]{1,0:T(8,128)(2,1)S(1)}, bf16[128,3072]{1,0:T(8,128)(2,1)}, u32[]{:S(2)}) copy-start(bf16[128,3072]{1,0:T(8,128)(2,1)} %get-tuple-element.14) | copy-start | bytes 2359300
  83.3 10.9 %copy-start.1 = (bf16[128,3072]{1,0:T(8,128)(2,1)S(1)}, bf16[128,3072]{1,0:T(8,128)(2,1)}, u32[]{:S(2)}) copy-start(bf16[128,3072]{1,0:T(8,128)(2,1)} %get-tuple-element.15) | copy-start | bytes 2359300
  94.2 9.5 %copy-start.3 = (bf16[16,3072]{1,0:T(8,128)(2,1)S(1)}, bf16[16,3072]{1,0:T(8,128)(2,1)}, u32[]{:S(2)}) copy-start(bf16[16,3072]{1,0:T(8,128)(2,1)} %get-tuple-element.20) | copy-start | bytes 294916
  94.2 10.2 %copy-start.2 = (bf16[16,3072]{1,0:T(8,128)(2,1)S(1)}, bf16[16,3072]{1,0:T(8,128)(2,1)}, u32[]{:S(2)}) copy-start(bf16[16,3072]{1,0:T(8,128)(2,1)} %get-tuple-element.21) | copy-start | bytes 294916

commit v2 on v1

--- a/solution.py
+++ b/solution.py
@@ -9,7 +9,7 @@
 
 gelu_scale = 0.7978845608028654
 gelu_cubic = 0.044715
-TILE = 256
+TILE = 768
 F32 = jnp.float32
 BF16 = jnp.bfloat16
 
@@ -35,14 +35,17 @@
 def kernel(
     n_row, n_col, chunk, part,
     x_ref, g_ref, w_in_hbm, w_out_hbm,
-    out_ref, gt_ref, xp, gp, hid, gpre,
-    w_in, w_out, terms_a, terms_b, land_a, land_b, slope, total, own_a, own_b,
-    pair_a, pair_b, sums_a, sums_b, last_a, last_b,
-    load_sem, ag_send, ag_recv, fw_send, fw_recv, rs_send, rs_recv, hg_send, hg_recv,
-    pr_send, pr_recv, zs_send, zs_recv,
+    out_ref, xp, gp, hid, gpre, *rest,
 ):
+    n_chip = n_col // 2
+    ready = rest[:n_chip]
+    (
+        w_in, w_out, terms_a, terms_b, land_a, land_b, slope, total, own_a, own_b,
+        pair_a, pair_b, sums, last,
+        load_sem, ag_send, ag_recv, fw_send, fw_recv, rs_send, rs_recv, hg_send, hg_recv,
+        pr_send, pr_recv, zs_send, zs_recv,
+    ) = rest[n_chip:]
     r, q = lax.axis_index("row"), lax.axis_index("col")
-    n_chip = n_col // 2
     z, core = q // 2, q % 2
     mate = z * 2 + (1 - core)
     n_tok, width = xp.shape
@@ -65,9 +68,8 @@
         return pltpu.make_async_copy(
             w_out_hbm.at[aligned(j, chunk), :], w_out.at[aligned(j, chunk), :], load_sem.at[1, j])
 
-    for which in range(2):
-        for j in range(n_chunk):
-            load(which, j).start()
+    for j in range(n_chunk):
+        load(0, j).start()
 
     barrier = pltpu.get_barrier_semaphore()
     for k in range(1, n_row):
@@ -102,10 +104,12 @@
         there = panels[a].at[aligned(z_at(n_chip - k) * 2 + (1 - core), rows_c)]
         return remote(there, there, fw_send.at[a, k], fw_recv.at[a, k], col=mate)
 
-    for a in range(2):
+    def start_panel(a):
         for k in range(1, n_chip):
             gather_out(a, k).start()
         forward_out(a, 0).start()
+
+    start_panel(0)
     for a in range(2):
         panels[a][aligned(q, rows_c), :] = blocks[a][...]
 
@@ -113,6 +117,10 @@
         for k in range(1, n_chip):
             gather_in(a, k).wait_recv()
             forward_out(a, k).start()
+        if a == 0:
+            start_panel(1)
+            for j in range(n_chunk):
+                load(1, j).start()
         for k in range(n_chip):
             forward_in(a, k).wait_recv()
 
@@ -175,20 +183,17 @@
 
     owns = (own_a, own_b)
     pairs = (pair_a, pair_b)
-    sums = (sums_a, sums_b)
-    lasts = (last_a, last_b)
-    results = (out_ref, gt_ref)
 
     def pair_out(a, h):
         cols = pl.ds(h * part, part)
         return remote(owns[a].at[1 - core, :, cols], pairs[a].at[:, cols],
                       pr_send.at[a, h], pr_recv.at[a, h], col=mate)
 
-    def chip_out(a, h, k):
+    def chip_out(h, k):
         cols = pl.ds(h * part, part)
         to = z_at(k)
-        return remote(sums[a].at[aligned(to, rows_c), cols], lasts[a].at[k - 1, :, cols],
-                      zs_send.at[a, h, k], zs_recv.at[a, h, k], col=to * 2 + core)
+        return remote(sums.at[aligned(to, rows_c), cols], last.at[k - 1, :, cols],
+                      zs_send.at[h, k], zs_recv.at[h, k], col=to * 2 + core)
 
     def second(a):
         def term(j, t):
@@ -239,19 +244,25 @@
         for h in range(n_part):
             cols = pl.ds(h * part, part)
             pair_out(a, h).wait_recv()
-            both = owns[a][core, :, cols].astype(F32) + pairs[a][:, cols].astype(F32)
-            sums[a][:, cols] = both.astype(BF16)
-            for k in range(1, n_chip):
-                chip_out(a, h, k).start()
-
-    def end(a):
+            if a == 0:
+                both = owns[a][core, :, cols].astype(F32) + pairs[a][:, cols].astype(F32)
+                sums[:, cols] = both.astype(BF16)
+                for k in range(1, n_chip):
+                    chip_out(h, k).start()
+            else:
+                for k in range(n_chip):
+                    rows = aligned(z_at(k), rows_c)
+                    both = owns[a][core, rows, cols].astype(F32) + pairs[a][rows, cols].astype(F32)
+                    ready[k][:, cols] = both.astype(BF16)
+
+    def end():
         for h in range(n_part):
             cols = pl.ds(h * part, part)
-            value = sums[a][aligned(z, rows_c), cols].astype(F32)
+            value = sums[aligned(z, rows_c), cols].astype(F32)
             for k in range(1, n_chip):
-                chip_out(a, h, k).wait_recv()
-                value = value + lasts[a][k - 1, :, cols].astype(F32)
-            results[a][:, cols] = value.astype(BF16)
+                chip_out(h, k).wait_recv()
+                value = value + last[k - 1, :, cols].astype(F32)
+            out_ref[:, cols] = value.astype(BF16)
 
     finish_panel(0)
     first(0)
@@ -261,8 +272,7 @@
     middle(1)
     second(0)
     second(1)
-    end(0)
-    end(1)
+    end()
 
     for a in range(2):
         for k in range(1, n_chip):
@@ -271,8 +281,6 @@
             forward_out(a, k).wait_send()
         for h in range(n_part):
             pair_out(a, h).wait_send()
-            for k in range(1, n_chip):
-                chip_out(a, h, k).wait_send()
 
         def sent(j, carry):
             for k in range(1, n_row):
@@ -281,6 +289,9 @@
             return carry
 
         lax.fori_loop(0, n_chunk, sent, 0)
+    for h in range(n_part):
+        for k in range(1, n_chip):
+            chip_out(h, k).wait_send()
 
 
 def exchange(n_row, n_col, tokens, w_in, w_out, grad_out):
@@ -300,12 +311,13 @@
     return pl.pallas_call(
         functools.partial(kernel, n_row, n_col, chunk, part),
         out_shape=(
-            shape((rows_c, width), BF16), shape((rows_c, width), BF16),
+            shape((rows_c, width), BF16),
             shape((n_tok, width), BF16), shape((n_tok, width), BF16),
             shape((n_tok, hidden_units), BF16), shape((n_tok, hidden_units), BF16),
+            *[shape((rows_c, width), BF16)] * n_chip,
         ),
         in_specs=[vmem, vmem, hbm, hbm],
-        out_specs=[vmem] * 6,
+        out_specs=[vmem] * (5 + n_chip),
         scratch_shapes=[
             pltpu.VMEM(w_in.shape, BF16), pltpu.VMEM(w_out.shape, BF16),
             *twice(n_tok, hidden_units),
@@ -314,14 +326,14 @@
             pltpu.VMEM((n_tok, width), F32),
             *twice(2, n_chip * rows_c, width),
             *twice(n_chip * rows_c, width),
-            *twice(n_chip * rows_c, width),
-            *twice(n_chip - 1, rows_c, width),
+            pltpu.VMEM((n_chip * rows_c, width), BF16),
+            pltpu.VMEM((n_chip - 1, rows_c, width), BF16),
             dma((2, n_chunk)),
             dma((2, n_chip)), dma((2, n_chip)), dma((2, n_chip)), dma((2, n_chip)),
             dma((2, n_chunk, n_row)), dma((2, n_chunk, n_row)),
             dma((2, n_chunk, n_row)), dma((2, n_chunk, n_row)),
             dma((2, n_part)), dma((2, n_part)),
-            dma((2, n_part, n_chip)), dma((2, n_part, n_chip)),
+            dma((n_part, n_chip)), dma((n_part, n_chip)),
         ],
         compiler_params=pltpu.CompilerParams(
             collective_id=0, has_side_effects=True, vmem_limit_bytes=60 * 1024 * 1024),
@@ -333,14 +345,52 @@
     )(tokens, grad_out, w_in, w_out)
 
 
+ROWS = 384
+COLS = 512
+
+
+def outer_kernel(xp, gpre, hid, gp, in_ref, out_ref):
+    for left, right, result in ((xp, gpre, in_ref), (hid, gp, out_ref)):
+        turned = left[...].T
+        for at in range(0, right.shape[1], COLS):
+            cols = pl.ds(at, min(COLS, right.shape[1] - at))
+            result[:, cols] = jnp.dot(
+                turned, right[:, cols], preferred_element_type=F32).astype(BF16)
+
+
+def outer(xp, gpre, hid, gp):
+    n_tok, width = xp.shape
+    side = hid.shape[1]
+    rows = ROWS * side // width
+    left = lambda size: pl.BlockSpec((n_tok, size), lambda i: (0, i))
+    right = lambda size: pl.BlockSpec((n_tok, size), lambda i: (0, 0))
+    return pl.pallas_call(
+        outer_kernel,
+        grid=(width // ROWS,),
+        out_shape=(jax.ShapeDtypeStruct((width, side), BF16), jax.ShapeDtypeStruct((side, width), BF16)),
+        in_specs=[left(ROWS), right(side), left(rows), right(width)],
+        out_specs=(pl.BlockSpec((ROWS, side), lambda i: (i, 0)), pl.BlockSpec((rows, width), lambda i: (i, 0))),
+        compiler_params=pltpu.CompilerParams(vmem_limit_bytes=61 * 1024 * 1024),
+        cost_estimate=pl.CostEstimate(
+            flops=4 * n_tok * width * side, bytes_accessed=4 * width * side, transcendentals=0),
+        name="outer",
+    )(xp, gpre, hid, gp)
+
+
 def per_device(n_row, n_col, tokens, w_in, w_out, grad_out):
-    block_out, grad_tokens, token_panel, grad_panel, hidden, grad_pre = exchange(
+    block_out, token_panel, grad_panel, hidden, grad_pre, *ready = exchange(
         n_row, n_col, tokens, w_in, w_out, grad_out)
-    grad_w_in = lax.dot_general(
-        token_panel, grad_pre, (((0,), (0,)), ((), ())), preferred_element_type=F32)
-    grad_w_out = lax.dot_general(
-        hidden, grad_panel, (((0,), (0,)), ((), ())), preferred_element_type=F32)
-    return (block_out, grad_tokens, grad_w_in.astype(BF16), grad_w_out.astype(BF16))
+    n_chip = n_col // 2
+    arrived = [
+        lax.ppermute(ready[k], "col", [
+            (z * 2 + core, (z + k) % n_chip * 2 + core) for z in range(n_chip) for core in range(2)])
+        for k in range(1, n_chip)
+    ]
+    grad_w_in, grad_w_out = outer(token_panel, grad_pre, hidden, grad_panel)
+    grad_tokens = ready[0].astype(F32)
+    for term in arrived:
+        grad_tokens = grad_tokens + term.astype(F32)
+    return (block_out, grad_tokens.astype(BF16), grad_w_in, grad_w_out)
 
 
 def solution(mesh):

time: 105 us -> 84.4 us (0.80)
  matrix products: 20.4 us -> 0 us
  Pallas kernels: 82.6 us -> 74.9 us
  starting transfers between devices: 0 us -> 5.5 us
  other arithmetic: 0 us -> 1.59 us
    pallas_call x1, Pallas kernels: 82.6 us -> 60.2 us  [exchange(): pl.pallas_call(functools.partial(kernel, n_row, n_col, chunk, part), out_...]
    dot_general x2 -> x0, matrix products: 20.4 us -> none  [the longest x1 10.9 us: per_device(): lax.dot_general(token_panel, grad_pre, (((0,), (0,)), ((), ())), preferre...]
    pallas_call x0 -> x1, Pallas kernels: none -> 14.7 us  [outer(): pl.pallas_call(outer_kernel, grid=(width // ROWS,), out_shape=(jax.ShapeD...]
    ppermute x0 -> x3, starting transfers between devices: none -> 5.5 us  [per_device(): lax.ppermute(ready[k], 'col', [(z * 2 + core, (z + k) % n_chip * 2 + core...]
    convert_element_type x0 -> x1, other arithmetic: none -> 1.59 us  [per_device(): return (block_out, grad_tokens.astype(BF16), grad_w_in, grad_w_out)]
  transfers between devices with their start and end apart: 0 -> 3, of which waited for: 0 -> 0; matrix products, arithmetic and copies ran while one was open for 0% -> 0% of each run, Pallas kernels for 0% -> 17%
where the time goes in v2:
time: 84.4 us; the launch traced here: 84.2 us
  Pallas kernels  74.9 us (89%)
  starting transfers between devices  5.5 us (7%)
  other arithmetic  1.59 us (2%)
  local copies, waits for them, and re-layouts  1.54 us (2%)
    pallas_call x1, Pallas kernels, exchange(): pl.pallas_call(functools.partial(kernel, n_row, n_col, chunk, part), out_...  60.2 us
    pallas_call x1, Pallas kernels, outer(): pl.pallas_call(outer_kernel, grid=(width // ROWS,), out_shape=(jax.ShapeD...  14.7 us
    ppermute x3, starting transfers between devices, per_device(): lax.ppermute(ready[k], 'col', [(z * 2 + core, (z + k) % n_chip * 2 + core...  5.5 us
  transfers between devices with their start and end apart: 3, of which 0 were waited for; matrix products, arithmetic and copies ran while one was open for 0% of the time, Pallas kernels for 17%

profile of v2, /device:TPU:0, one launch (start us, length us, event | category | flops | bytes accessed | tf_op | source)
XLA Modules:
  0.0 84.2 jit_solution(6586533857320681599)
XLA Ops:
  0.6 60.2 %exchange.1 = (bf16[16,3072]{1,0:T(8,128)(2,1)}, bf16[128,3072]{1,0:T(8,128)(2,1)}, bf16[128,3072]{1,0:T(8,128)(2,1)}, bf16[128,3072]{1,0:T(8,128)(2,1)}, bf16[1...) custom-call(bf16[16,3072]{1,0:T(8,128)(2,1)} %x_ref.1, ...), custom_call_target="tpu_custom_call" | custom-call | flops 9663676416 | bytes 37748736 | tf_op jit(solution)/shard_map/exchange/pallas_call | solution.py:311
  60.8 2.2 %collective-permute-start = (bf16[16,3072]{1,0:T(8,128)(2,1)}, bf16[16,3072]{1,0:T(8,128)(2,1)S(1)}, u32[]{:S(2)}, u32[]{:S(2)}) collective-permute-start(bf16[16,3072]{1,0:T(8,128)(2,1)} %get-tuple-element.17), channel_id=1, source_target_pairs={{0,2},{1,3},{2,4},{3,5},{4,6},{5,7},{6,0},{7,1},{8,10},{9,11},{10,... | collective-permute-start | bytes 294920 | tf_op jit(solution)/shard_map/ppermute | solution.py:385
  63.0 3.3 %collective-permute-start.1 = (bf16[16,3072]{1,0:T(8,128)(2,1)}, bf16[16,3072]{1,0:T(8,128)(2,1)S(1)}, u32[]{:S(2)}, u32[]{:S(2)}) collective-permute-start(bf16[16,3072]{1,0:T(8,128)(2,1)} %get-tuple-element.18), channel_id=1, source_target_pairs={{0,4},{1,5},{2,6},{3,7},{4,0},{5,1},{6,2},{7,3},{8,12},{9,13},{10,... | collective-permute-start | bytes 294920 | tf_op jit(solution)/shard_map/ppermute | solution.py:385
  66.3 0.0 collective-permute-start.2
  66.3 14.7 %outer.1 = (bf16[3072,3072]{1,0:T(8,128)(2,1)}, bf16[3072,3072]{1,0:T(8,128)(2,1)}) custom-call(bf16[128,3072]{1,0:T(8,128)(2,1)} %get-tuple-element.20.xp, bf16[128,3072]{1,0:T(8,128)(2,1)} %get-tuple-element.21.gpre, bf16[128,3072]{1,0:T(8,128)(2,1)} %get-tuple-element.22.hid, bf16[128,3072]{1,0:T(8,128)(2,1)} %get-tuple-element.23.gp), custom_call_target="tpu_custom_call" | custom-call | flops 4831838208 | bytes 37748736 | tf_op jit(solution)/shard_map/outer/pallas_call | solution.py:367
  81.0 0.0 collective-permute-done
  81.0 0.0 collective-permute-done.1
  81.0 0.0 collective-permute-done.2
  81.0 1.6 %add_convert_fusion = bf16[16,3072]{1,0:T(8,128)(2,1)} fusion(bf16[16,3072]{1,0:T(8,128)(2,1)S(1)} %collective-permute-done.2, bf16[16,3072]{1,0:T(8,128)(2,1)S(1)} %collective-permute-done.1, bf16[16,3072]{1,0:T(8,128)(2,1)S(1)} %collective-permute-done, bf16[16,3072]{1,0:T(8,128)(2,1)} %get-tuple-element.16), kind=kLoop, calls=%fused_computation | loop fusion | flops 393216 | bytes 491520 | tf_op jit(solution)/shard_map/convert_element_type | solution.py:393
  82.6 1.5 %copy.9 = bf16[16,3072]{1,0:T(8,128)(2,1)} copy(bf16[16,3072]{1,0:T(8,128)(2,1)} %get-tuple-element.30) | data formatting | bytes 196608
Async XLA Ops:
  60.8 20.2 %collective-permute-start = (bf16[16,3072]{1,0:T(8,128)(2,1)}, bf16[16,3072]{1,0:T(8,128)(2,1)S(1)}, u32[]{:S(2)}, u32[]{:S(2)}) collective-permute-start(bf16[16,3072]{1,0:T(8,128)(2,1)} %get-tuple-element.17), channel_id=1, source_target_pairs={{0,2},{1,3},{2,4},{3,5},{4,6},{5,7},{6,0},{7,1},{8,10},{9,11},{10,... | collective-permute-start | bytes 294920 | tf_op jit(solution)/shard_map/ppermute | solution.py:385
  63.0 18.0 %collective-permute-start.1 = (bf16[16,3072]{1,0:T(8,128)(2,1)}, bf16[16,3072]{1,0:T(8,128)(2,1)S(1)}, u32[]{:S(2)}, u32[]{:S(2)}) collective-permute-start(bf16[16,3072]{1,0:T(8,128)(2,1)} %get-tuple-element.18), channel_id=1, source_target_pairs={{0,4},{1,5},{2,6},{3,7},{4,0},{5,1},{6,2},{7,3},{8,12},{9,13},{10,... | collective-permute-start | bytes 294920 | tf_op jit(solution)/shard_map/ppermute | solution.py:385
  66.3 14.7 %collective-permute-start.2 = (bf16[16,3072]{1,0:T(8,128)(2,1)}, bf16[16,3072]{1,0:T(8,128)(2,1)S(1)}, u32[]{:S(2)}, u32[]{:S(2)}) collective-permute-start(bf16[16,3072]{1,0:T(8,128)(2,1)} %get-tuple-element.19), channel_id=1, source_target_pairs={{0,6},{1,7},{2,0},{3,1},{4,2},{5,3},{6,4},{7,5},{8,14},{9,15},{10,... | collective-permute-start | bytes 294920 | tf_op jit(solution)/shard_map/ppermute | solution.py:385

commit v3 on v2

--- a/solution.py
+++ b/solution.py
@@ -158,28 +158,26 @@
             lax.fori_loop(0, chunk // TILE, per_tile, 0)
             for k in range(1, n_row):
                 scatter_out(a, j, k).start()
+            if a == 1:
+                middle(0, j)
             return carry
 
         lax.fori_loop(0, n_chunk, per_chunk, 0)
 
-    def middle(a):
-        def per_chunk(j, carry):
-            cols = aligned(j, chunk)
-            total_here = terms[a][aligned(r, rows_r), cols].astype(F32)
-            for k in range(1, n_row):
-                scatter_out(a, j, k).wait_recv()
-                total_here = total_here + lands[a][k - 1, :, cols].astype(F32)
-            if a == 0:
-                value, gradient = gelu_pair(total_here)
-                slope[:, cols] = gradient
-            else:
-                value = total_here * slope[:, cols]
-            fulls[a][aligned(r, rows_r), cols] = value.astype(BF16)
-            for k in range(1, n_row):
-                spread_out(a, j, k).start()
-            return carry
-
-        lax.fori_loop(0, n_chunk, per_chunk, 0)
+    def middle(a, j):
+        cols = aligned(j, chunk)
+        total_here = terms[a][aligned(r, rows_r), cols].astype(F32)
+        for k in range(1, n_row):
+            scatter_out(a, j, k).wait_recv()
+            total_here = total_here + lands[a][k - 1, :, cols].astype(F32)
+        if a == 0:
+            value, gradient = gelu_pair(total_here)
+            slope[:, cols] = gradient
+        else:
+            value = total_here * slope[:, cols]
+        fulls[a][aligned(r, rows_r), cols] = value.astype(BF16)
+        for k in range(1, n_row):
+            spread_out(a, j, k).start()
 
     owns = (own_a, own_b)
     pairs = (pair_a, pair_b)
@@ -268,8 +266,12 @@
     first(0)
     finish_panel(1)
     first(1)
-    middle(0)
-    middle(1)
+
+    def middle_one(j, carry):
+        middle(1, j)
+        return carry
+
+    lax.fori_loop(0, n_chunk, middle_one, 0)
     second(0)
     second(1)
     end()

time: 84.4 us -> 87.1 us (1.032)
  Pallas kernels: 74.9 us -> 77.8 us
    pallas_call x1, Pallas kernels: 60.2 us -> 63.1 us  [exchange(): pl.pallas_call(functools.partial(kernel, n_row, n_col, chunk, part), out_...]
where the time goes in v3:
time: 87.1 us; the launch traced here: 86.8 us
  Pallas kernels  77.8 us (89%)
  starting transfers between devices  5.26 us (6%)
  other arithmetic  1.59 us (2%)
  local copies, waits for them, and re-layouts  1.54 us (2%)
    pallas_call x1, Pallas kernels, exchange(): pl.pallas_call(functools.partial(kernel, n_row, n_col, chunk, part), out_...  63.1 us
    pallas_call x1, Pallas kernels, outer(): pl.pallas_call(outer_kernel, grid=(width // ROWS,), out_shape=(jax.ShapeD...  14.7 us
    ppermute x3, starting transfers between devices, per_device(): lax.ppermute(ready[k], 'col', [(z * 2 + core, (z + k) % n_chip * 2 + core...  5.26 us
  transfers between devices with their start and end apart: 3, of which 0 were waited for; matrix products, arithmetic and copies ran while one was open for 0% of the time, Pallas kernels for 17%

profile of v3, /device:TPU:0, one launch (start us, length us, event | category | flops | bytes accessed | tf_op | source)
XLA Modules:
  0.0 86.8 jit_solution(196377962898195924)
XLA Ops:
  0.6 63.1 %exchange.1 = (bf16[16,3072]{1,0:T(8,128)(2,1)}, bf16[128,3072]{1,0:T(8,128)(2,1)}, bf16[128,3072]{1,0:T(8,128)(2,1)}, bf16[128,3072]{1,0:T(8,128)(2,1)}, bf16[1...) custom-call(bf16[16,3072]{1,0:T(8,128)(2,1)} %x_ref.1, ...), custom_call_target="tpu_custom_call" | custom-call | flops 9663676416 | bytes 37748736 | tf_op jit(solution)/shard_map/exchange/pallas_call | solution.py:313
  63.7 2.0 %collective-permute-start = (bf16[16,3072]{1,0:T(8,128)(2,1)}, bf16[16,3072]{1,0:T(8,128)(2,1)S(1)}, u32[]{:S(2)}, u32[]{:S(2)}) collective-permute-start(bf16[16,3072]{1,0:T(8,128)(2,1)} %get-tuple-element.17), channel_id=1, source_target_pairs={{0,2},{1,3},{2,4},{3,5},{4,6},{5,7},{6,0},{7,1},{8,10},{9,11},{10,... | collective-permute-start | bytes 294920 | tf_op jit(solution)/shard_map/ppermute | solution.py:387
  65.7 2.9 %collective-permute-start.1 = (bf16[16,3072]{1,0:T(8,128)(2,1)}, bf16[16,3072]{1,0:T(8,128)(2,1)S(1)}, u32[]{:S(2)}, u32[]{:S(2)}) collective-permute-start(bf16[16,3072]{1,0:T(8,128)(2,1)} %get-tuple-element.18), channel_id=1, source_target_pairs={{0,4},{1,5},{2,6},{3,7},{4,0},{5,1},{6,2},{7,3},{8,12},{9,13},{10,... | collective-permute-start | bytes 294920 | tf_op jit(solution)/shard_map/ppermute | solution.py:387
  68.7 0.3 collective-permute-start.2
  69.0 14.7 %outer.1 = (bf16[3072,3072]{1,0:T(8,128)(2,1)}, bf16[3072,3072]{1,0:T(8,128)(2,1)}) custom-call(bf16[128,3072]{1,0:T(8,128)(2,1)} %get-tuple-element.20.xp, bf16[128,3072]{1,0:T(8,128)(2,1)} %get-tuple-element.21.gpre, bf16[128,3072]{1,0:T(8,128)(2,1)} %get-tuple-element.22.hid, bf16[128,3072]{1,0:T(8,128)(2,1)} %get-tuple-element.23.gp), custom_call_target="tpu_custom_call" | custom-call | flops 4831838208 | bytes 37748736 | tf_op jit(solution)/shard_map/outer/pallas_call | solution.py:369
  83.7 0.0 collective-permute-done
  83.7 0.0 collective-permute-done.1
  83.7 0.0 collective-permute-done.2
  83.7 1.6 %add_convert_fusion = bf16[16,3072]{1,0:T(8,128)(2,1)} fusion(bf16[16,3072]{1,0:T(8,128)(2,1)S(1)} %collective-permute-done.2, bf16[16,3072]{1,0:T(8,128)(2,1)S(1)} %collective-permute-done.1, bf16[16,3072]{1,0:T(8,128)(2,1)S(1)} %collective-permute-done, bf16[16,3072]{1,0:T(8,128)(2,1)} %get-tuple-element.16), kind=kLoop, calls=%fused_computation | loop fusion | flops 393216 | bytes 491520 | tf_op jit(solution)/shard_map/convert_element_type | solution.py:395
  85.3 1.5 %copy.9 = bf16[16,3072]{1,0:T(8,128)(2,1)} copy(bf16[16,3072]{1,0:T(8,128)(2,1)} %get-tuple-element.30) | data formatting | bytes 196608
Async XLA Ops:
  63.7 20.0 %collective-permute-start = (bf16[16,3072]{1,0:T(8,128)(2,1)}, bf16[16,3072]{1,0:T(8,128)(2,1)S(1)}, u32[]{:S(2)}, u32[]{:S(2)}) collective-permute-start(bf16[16,3072]{1,0:T(8,128)(2,1)} %get-tuple-element.17), channel_id=1, source_target_pairs={{0,2},{1,3},{2,4},{3,5},{4,6},{5,7},{6,0},{7,1},{8,10},{9,11},{10,... | collective-permute-start | bytes 294920 | tf_op jit(solution)/shard_map/ppermute | solution.py:387
  65.7 18.0 %collective-permute-start.1 = (bf16[16,3072]{1,0:T(8,128)(2,1)}, bf16[16,3072]{1,0:T(8,128)(2,1)S(1)}, u32[]{:S(2)}, u32[]{:S(2)}) collective-permute-start(bf16[16,3072]{1,0:T(8,128)(2,1)} %get-tuple-element.18), channel_id=1, source_target_pairs={{0,4},{1,5},{2,6},{3,7},{4,0},{5,1},{6,2},{7,3},{8,12},{9,13},{10,... | collective-permute-start | bytes 294920 | tf_op jit(solution)/shard_map/ppermute | solution.py:387
  68.7 15.0 %collective-permute-start.2 = (bf16[16,3072]{1,0:T(8,128)(2,1)}, bf16[16,3072]{1,0:T(8,128)(2,1)S(1)}, u32[]{:S(2)}, u32[]{:S(2)}) collective-permute-start(bf16[16,3072]{1,0:T(8,128)(2,1)} %get-tuple-element.19), channel_id=1, source_target_pairs={{0,6},{1,7},{2,0},{3,1},{4,2},{5,3},{6,4},{7,5},{8,14},{9,15},{10,... | collective-permute-start | bytes 294920 | tf_op jit(solution)/shard_map/ppermute | solution.py:387
